TPU v7x, 32 devices: a whole 2x2x4 slice. The times are simulated.
32 devices in a mesh: branch: 2 (over y), axial: 8 (over z, x), sub: 2 (over core).
Axes of the slice: x: 2, y: 2, z: 4, core: 2. Of those that a mesh axis runs over, the one named last changes fastest.
Arguments:
- lineup_embedding: bfloat16 [32, 32, 256], P(('branch', 'sub'), 'axial'), may hold values from -6 to 6
- pair_features: bfloat16 [32, 32, 128], P('axial', ('branch', 'sub')), may hold values from -6 to 6
- lineup_entry_keep: int32 [32], replicated, may hold values 0 or 1
- residue_mask: int32 [32], replicated, may hold values 0 or 1
- residue_chain_index: int32 [32], replicated, may hold values from 0 to 3, never falling along the last dimension, each value on 1 to 16 neighbouring positions
- intra_chain_bias: float32 [8], replicated, may hold values from -4 to 4
- pair_bias_weight: bfloat16 [128, 8], replicated, may hold values from -0.5 to 0.5
- attention_weight: bfloat16 [256, 1024], replicated, may hold values from -6 to 6
- final_linear_matrix: bfloat16 [256, 256], replicated, may hold values from -0.375 to 0.375
- tensor_side_matrix: bfloat16 [256, 64], replicated, may hold values from -0.375 to 0.375
- outer_project_weight: bfloat16 [1024, 128], replicated, may hold values from -1 to 1
Outputs:
- alignment_output: bfloat16 [32, 32, 256], P(('branch', 'sub'), 'axial')
- pair_delta_update: bfloat16 [32, 32, 128], P('axial', ('branch', 'sub'))
Inputs may be any that keep to these rules, and one draw needn't show every extreme that they name: `residue_chain_index`: chain numbers never fall along the residues; at most 4 chains, one of 16 residues.
All inputs are finite; a program needn't handle non-finite values.
Results may differ from a plain program's by a relative error of at most 0.0094.
Values may be sent and summed in bfloat16 or wider, within the bound.
A program may use at most 64 MiB of HBM per device.

v0:
```python
import jax
import jax.numpy as jnp
from jax import lax
from jax.sharding import PartitionSpec as P

HEAD_COUNT = 8
HEAD_SPAN = 32


def normalize_layer(values):
    values = values.astype(jnp.float32)
    average = jnp.mean(values, axis=-1, keepdims=True)
    centered = values - average
    variance = jnp.mean(centered * centered, axis=-1, keepdims=True)
    return centered * lax.rsqrt(variance + 1e-05)


def pair_bias(pair_features, chain_rows, chain_cols, intra_chain_bias, pair_bias_weight):
    standardized_embedding = normalize_layer(pair_features).astype(jnp.bfloat16)
    row_total, col_total, channels = standardized_embedding.shape
    biased = jnp.dot(
        standardized_embedding.reshape(row_total * col_total, channels),
        pair_bias_weight,
        preferred_element_type=jnp.float32,
    )
    biased = biased.reshape(row_total, col_total, -1)
    same_chain = (chain_rows[:, None] == chain_cols[None, :]).astype(jnp.float32)
    biased = biased + same_chain[:, :, None] * intra_chain_bias[None, None, :]
    return jnp.transpose(biased, (2, 0, 1)).astype(jnp.bfloat16)


def attend(
    row_values,
    normed_keys,
    normed_queries,
    bias,
    key_valid_mask,
    attention_weight,
    final_linear_matrix,
):
    seq_total, key_total, _ = normed_keys.shape
    query_total = normed_queries.shape[1]
    single_head_span = HEAD_COUNT * HEAD_SPAN
    key_values = jnp.einsum(
        "skc,cf->skf",
        normed_keys,
        attention_weight[:, single_head_span : 3 * single_head_span],
        preferred_element_type=jnp.float32,
    ).astype(jnp.bfloat16)
    w_query_gate = jnp.concatenate(
        (attention_weight[:, :single_head_span], attention_weight[:, 3 * single_head_span :]),
        axis=1,
    )
    fronts = jnp.einsum(
        "sqc,cf->sqf", normed_queries, w_query_gate, preferred_element_type=jnp.float32
    ).astype(jnp.bfloat16)
    key_heads = key_values.reshape(seq_total, key_total, 2, HEAD_COUNT, HEAD_SPAN).transpose(
        2, 3, 0, 1, 4
    )
    query_heads = fronts.reshape(seq_total, query_total, 2, HEAD_COUNT, HEAD_SPAN).transpose(
        2, 3, 0, 1, 4
    )
    scaling = 1.0 / HEAD_SPAN**0.5

    def one_head(operands):
        queries, key_side, val_side, bias_head = operands
        scores = jnp.einsum("sqd,skd->sqk", queries, key_side, preferred_element_type=jnp.float32)
        scores = (
            scores * scaling
            + bias_head.astype(jnp.float32)[None, :, :]
            + key_valid_mask[None, None, :]
        )
        maximum = jnp.max(scores, axis=-1, keepdims=True)
        expsum = jnp.exp(scores - maximum)
        weights = (expsum / jnp.sum(expsum, axis=-1, keepdims=True)).astype(jnp.bfloat16)
        return jnp.einsum("sqk,skd->sqd", weights, val_side, preferred_element_type=jnp.float32)

    attended = lax.map(one_head, (query_heads[0], key_heads[0], key_heads[1], bias))
    attended = attended.transpose(1, 2, 0, 3).reshape(seq_total, query_total, single_head_span)
    gate_side = (
        query_heads[1]
        .transpose(1, 2, 0, 3)
        .reshape(seq_total, query_total, single_head_span)
        .astype(jnp.float32)
    )
    gated_rows = (attended * jax.nn.sigmoid(gate_side)).astype(jnp.bfloat16)
    update = jnp.einsum(
        "sqf,fc->sqc", gated_rows, final_linear_matrix, preferred_element_type=jnp.float32
    )
    return (row_values.astype(jnp.float32) + update).astype(jnp.bfloat16)


def attend_whole(
    sequence_rows, combined_bias, key_valid_mask, attention_weight, final_linear_matrix
):
    standardized_embedding = normalize_layer(sequence_rows).astype(jnp.bfloat16)
    return attend(
        sequence_rows,
        standardized_embedding,
        standardized_embedding,
        combined_bias,
        key_valid_mask,
        attention_weight,
        final_linear_matrix,
    )


def outer_product_input(alignment_block, sequence_mask, position_mask, tensor_side_matrix):
    standardized_embedding = normalize_layer(alignment_block).astype(jnp.bfloat16)
    seq_total, res_total, feat_total = standardized_embedding.shape
    values = jnp.dot(
        standardized_embedding.reshape(seq_total * res_total, feat_total),
        tensor_side_matrix,
        preferred_element_type=jnp.float32,
    )
    values = values.reshape(seq_total, res_total, -1)
    weight = sequence_mask.astype(jnp.float32)[:, None] * position_mask.astype(jnp.float32)[None, :]
    return (values * weight[:, :, None]).astype(jnp.bfloat16)


def shards(
    lineup_embedding,
    pair_features,
    lineup_entry_keep,
    residue_mask,
    residue_chain_index,
    intra_chain_bias,
    pair_bias_weight,
    attention_weight,
    final_linear_matrix,
    tensor_side_matrix,
    outer_project_weight,
):
    group_index = lax.axis_index("branch") * lax.axis_size("sub") + lax.axis_index("sub")
    axial_index = lax.axis_index("axial")
    local_res = pair_features.shape[0]
    local_cols = pair_features.shape[1]
    sequence_group = lineup_embedding.shape[0]
    row_start = axial_index * local_res
    col_start = group_index * local_cols
    chain_rows = lax.dynamic_slice_in_dim(residue_chain_index, row_start, local_res)
    chain_cols = lax.dynamic_slice_in_dim(residue_chain_index, col_start, local_cols)
    local_bias = pair_bias(
        pair_features, chain_rows, chain_cols, intra_chain_bias, pair_bias_weight
    )
    key_valid_mask = (residue_mask.astype(jnp.float32) - 1.0) * 1000000000.0
    sequence_rows = lax.all_to_all(
        lineup_embedding, "axial", split_axis=0, concat_axis=1, tiled=True
    )
    partial_bias = lax.all_gather(local_bias, ("branch", "sub"), axis=2, tiled=True)
    combined_bias = lax.all_gather(partial_bias, "axial", axis=1, tiled=True)
    updated = attend_whole(
        sequence_rows, combined_bias, key_valid_mask, attention_weight, final_linear_matrix
    )
    pos_rows = lax.dynamic_slice_in_dim(residue_mask, row_start, local_res)
    pos_cols = lax.dynamic_slice_in_dim(residue_mask, col_start, local_cols)
    back_rows = lax.all_to_all(updated, "axial", split_axis=1, concat_axis=0, tiled=True)
    sequence_mask = lax.dynamic_slice_in_dim(
        lineup_entry_keep, group_index * sequence_group, sequence_group
    )
    factor_rows = outer_product_input(back_rows, sequence_mask, pos_rows, tensor_side_matrix)
    factor_width = factor_rows.shape[2] // 2
    left_flat = factor_rows[:, :, :factor_width].reshape(sequence_group, local_res * factor_width)
    right_all = lax.all_gather(factor_rows[:, :, factor_width:], "axial", axis=1, tiled=True)
    row_count = lax.axis_size(("branch", "sub")) * local_cols
    chosen = right_all
    chosen = chosen.reshape(sequence_group, row_count * factor_width)
    outer_sum = lax.dot_general(
        left_flat, chosen, (((0,), (0,)), ((), ())), preferred_element_type=jnp.float32
    )
    outer_sum = outer_sum.astype(jnp.bfloat16)
    arranged = outer_sum.reshape(local_res, factor_width, row_count, factor_width).transpose(
        2, 0, 1, 3
    )
    arranged = arranged.reshape(row_count * local_res, factor_width * factor_width)
    opm_total = lax.psum_scatter(
        jnp.dot(arranged, outer_project_weight, preferred_element_type=jnp.float32).reshape(
            row_count, local_res, -1
        ),
        ("branch", "sub"),
        scatter_dimension=0,
        tiled=True,
    )
    pair_sums = jnp.transpose(opm_total, (1, 0, 2))
    seq_count = jnp.sum(lineup_entry_keep.astype(jnp.float32))
    counted = (
        seq_count * pos_rows.astype(jnp.float32)[:, None] * pos_cols.astype(jnp.float32)[None, :]
    )
    pair_delta_update = (pair_sums / jnp.maximum(counted, 1.0)[:, :, None]).astype(jnp.bfloat16)
    return (back_rows, pair_delta_update)


def solution(mesh):
    in_specs = (
        P(("branch", "sub"), "axial", None),
        P("axial", ("branch", "sub"), None),
        P(),
        P(),
        P(),
        P(),
        P(),
        P(),
        P(),
        P(),
        P(),
    )
    out_specs = (P(("branch", "sub"), "axial", None), P("axial", ("branch", "sub"), None))
    return jax.shard_map(shards, mesh=mesh, in_specs=in_specs, out_specs=out_specs, check_vma=False)
```

profile of v0, /device:TPU:0, one launch (start us, length us, event | category | flops | bytes accessed | tf_op | source)
XLA Modules:
  0.0 137.3 jit_solution(8945288473982829938)
XLA Ops:
  7.2 7.4 %all-to-all-start = ((bf16[8,4,256]{2,1,0:T(4,128)(2,1)}), bf16[8,4,256]{2,1,0:T(4,128)(2,1)S(1)}, u32[]{:S(2)}, u32[]{:S(2)}) async-start(bf16[8,4,256]{2,1,0:T(4,128)(2,1)} %param.13), calls=%async_computation | async-start | bytes 32768 | tf_op jit(solution)/shard_map/all_to_all | solution.py:147
  14.6 0.6 copy-done.8
  15.2 0.6 convert_reduce_fusion.3
  15.9 0.6 copy-done.9
  16.6 0.1 convert_reduce_fusion.1
  16.7 0.2 fusion.30
  16.9 1.0 fusion.40
  18.0 0.6 copy-done.5
  18.6 0.7 broadcast_multiply_fusion.3
  19.4 0.6 copy-done.7
  20.0 0.2 fusion.17
  20.2 5.2 %all_gather.9 = bf16[8,4,32]{0,2,1:T(8,128)(2,1)S(1)} all-gather(bf16[8,4,8]{0,2,1:T(8,128)(2,1)S(1)} %fusion.17), channel_id=1, replica_groups=mesh['branch'=2,'axial'=8,'sub'=2] {'branch','sub'}, dimensions={2}, use_global_device_ids=true | all-gather | bytes 2560 | tf_op jit(solution)/shard_map/all_gather | solution.py:150
  25.4 0.1 copy.41
  25.5 31.0 %all_gather.10 = bf16[8,32,32]{2,0,1:T(8,128)(2,1)S(1)} all-gather(bf16[8,4,32]{2,0,1:T(8,128)(2,1)S(1)} %copy.41), channel_id=1, replica_groups=mesh['branch'=2,'axial'=8,'sub'=2] {'axial'}, dimensions={1}, use_global_device_ids=true | all-gather | bytes 18432 | tf_op jit(solution)/shard_map/all_gather | solution.py:151
  56.5 0.1 copy.43
  56.6 0.1 convert_reduce_fusion.2
  56.7 0.1 div.46
  56.8 0.2 multiply_reduce_fusion.1
  57.0 0.2 convolution_convert_fusion.1
  57.2 0.2 convolution_convert_fusion.2
  57.4 0.1 reshape.351
  57.6 0.1 reshape.352
  57.8 3.0 %while.10 = (s32[]{:T(128)}, f32[8,1,32,32]{3,2,1,0:T(8,128)S(1)}, bf16[8,1,32,32]{3,2,1,0:T(8,128)(2,1)S(1)}, bf16[8,1,32,32]{3,2,1,0:T(8,128)(2,1)S(1)}, bf16[...) while((s32[]{:T(128)}, f32[8,1,32,32]{3,2,1,0:T(8,128)S(1)}, ...), condition=%wide.region_7.8_spmd, body=%wide.region_4.7_spmd.sunk | while | flops 141250 | bytes 78293 | solution.py:78
  57.9 0.1 fusion.52
  58.0 0.2 fusion.54
  58.2 0.2 fusion.52
  58.4 0.2 fusion.54
  58.6 0.2 fusion.52
  58.8 0.2 fusion.54
  59.0 0.2 fusion.52
  59.1 0.2 fusion.54
  59.3 0.2 fusion.52
  59.5 0.2 fusion.54
  59.7 0.2 fusion.52
  59.9 0.2 fusion.54
  60.1 0.2 fusion.52
  60.3 0.2 fusion.54
  60.4 0.2 fusion.52
  60.6 0.2 fusion.54
  60.9 0.1 reshape.366
  61.0 0.8 copy-done.2
  61.8 0.1 fusion.15
  62.0 0.5 broadcast.222
  62.5 0.7 reduce.13
  63.2 0.6 reshape.373
  63.8 5.4 %all-to-all-start.1 = ((bf16[8,2,512]{2,1,0:T(2,128)(2,1)}), bf16[8,2,512]{2,1,0:T(2,128)(2,1)S(1)}, u32[]{:S(2)}, u32[]{:S(2)}) async-start(bf16[8,2,512]{2,1,0:T(2,128)(2,1)} %reshape.373), calls=%async_computation.1 | async-start | bytes 32768 | tf_op jit(solution)/shard_map/all_to_all | solution.py:157
  69.4 6.5 %all-to-all-done.1 = bf16[8,2,512]{2,1,0:T(2,128)(2,1)S(1)} async-done(((bf16[8,2,512]{2,1,0:T(2,128)(2,1)}), bf16[8,2,512]{2,1,0:T(2,128)(2,1)S(1)}, u32[]{:S(2)}, u32[]{:S(2)}) %all-to-all-start.1) | async-done | bytes 16416 | tf_op jit(solution)/shard_map/all_to_all | solution.py:157
  75.9 0.3 convert_reduce_fusion
  76.2 0.1 bitcast_reduce_fusion
  76.3 0.5 multiply_reduce_fusion
  76.9 0.1 rsqrt.30
  77.0 0.1 multiply_convert_fusion
  77.1 0.5 copy-done.3
  77.6 0.1 copy-done.6
  77.9 30.6 %all_gather.11 = bf16[8,32,32]{2,0,1:T(8,128)(2,1)S(1)} all-gather(bf16[8,4,32]{2,0,1:T(8,128)(2,1)S(1)} %get-tuple-element.90), channel_id=1, replica_groups=mesh['branch'=2,'axial'=8,'sub'=2] {'axial'}, dimensions={1}, use_global_device_ids=true | all-gather | bytes 18432 | tf_op jit(solution)/shard_map/all_gather | solution.py:164
  108.5 0.1 reshape.355
  108.6 0.1 reshape.354
  108.7 0.3 convolution_convert_fusion
  109.0 0.8 reshape.356
  109.7 0.4 copy.49
  110.1 1.1 dot_general.38
  111.3 0.8 fusion.22
  112.2 16.9 %reduce-scatter.2.cloned.1.call-done = f32[8,4,128]{2,0,1:T(8,128)} async-done(((f32[32,4,128]{2,0,1:T(8,128)}), f32[8,4,128]{2,0,1:T(8,128)}) %reduce-scatter.2.cloned.1.call-update) | async-done | bytes 16400 | tf_op jit(solution)/shard_map/reduce_scatter | solution.py:176
  129.1 1.4 %fusion.32 = bf16[4,8,128]{2,1,0:T(8,128)(2,1)} fusion(f32[8,4,128]{2,0,1:T(8,128)} %reduce-scatter.2.cloned.1.call-done, f32[4,8]{1,0:T(4,128)S(1)} %multiply_maximum_fusion), kind=kLoop, calls=%fused_computation.56 | loop fusion | flops 8192 | bytes 24704 | tf_op jit(solution)/shard_map/convert_element_type | solution.py:189
  (57 shorter events, 1.4 us)
Async XLA Ops:
  7.2 104.1 %copy-start = (bf16[1024,128]{1,0:T(8,128)(2,1)S(1)}, bf16[1024,128]{1,0:T(8,128)(2,1)}, u32[]{:S(2)}) copy-start(bf16[1024,128]{1,0:T(8,128)(2,1)} %param.23) | copy-start | bytes 786436
  7.2 49.5 %all-to-all-start = ((bf16[8,4,256]{2,1,0:T(4,128)(2,1)}), bf16[8,4,256]{2,1,0:T(4,128)(2,1)S(1)}, u32[]{:S(2)}, u32[]{:S(2)}) async-start(bf16[8,4,256]{2,1,0:T(4,128)(2,1)} %param.13), calls=%async_computation | async-start | bytes 32768 | tf_op jit(solution)/shard_map/all_to_all | solution.py:147
  14.6 0.7 copy-start.8
  14.6 2.1 %copy-start.4 = (bf16[4,8,128]{2,1,0:T(8,128)(2,1)S(1)}, bf16[4,8,128]{2,1,0:T(8,128)(2,1)}, u32[]{:S(2)}) copy-start(bf16[4,8,128]{2,1,0:T(8,128)(2,1)} %param.14) | copy-start | bytes 24580
  15.8 0.7 copy-start.9
  16.9 40.1 %copy-start.1 = (bf16[256,1024]{1,0:T(8,128)(2,1)S(1)}, bf16[256,1024]{1,0:T(8,128)(2,1)}, u32[]{:S(2)}) copy-start(bf16[256,1024]{1,0:T(8,128)(2,1)} %param.20) | copy-start | bytes 1572868
  18.0 0.7 copy-start.5
  19.3 0.7 copy-start.7
  19.3 0.7 copy-start.10
  60.9 0.9 copy-start.2
  63.8 12.0 %all-to-all-start.1 = ((bf16[8,2,512]{2,1,0:T(2,128)(2,1)}), bf16[8,2,512]{2,1,0:T(2,128)(2,1)S(1)}, u32[]{:S(2)}, u32[]{:S(2)}) async-start(bf16[8,2,512]{2,1,0:T(2,128)(2,1)} %reshape.373), calls=%async_computation.1 | async-start | bytes 32768 | tf_op jit(solution)/shard_map/all_to_all | solution.py:157
  69.3 59.8 %reduce-scatter.2.cloned.1.call-start = ((), (), s32[]{:S(2)}) async-start(), calls=%async_computation.3 | async-start | bytes 81920 | tf_op jit(solution)/shard_map/reduce_scatter | solution.py:176
  77.0 0.8 copy-start.6
  77.0 0.6 copy-start.3
Sparse Core Ops, SparseCore 0:
  112.2 16.7 reduce-scatter.1
where the time goes:
time: 138 us; the launch traced here: 137 us
  blocking collectives  66.8 us (48%)
  waiting for transfers between devices  23.4 us (17%)
  between operations  14.3 us (10%)
  starting transfers between devices  12.9 us (9%)
  local copies, waits for them, and re-layouts  9.87 us (7%)
  other arithmetic  5.54 us (4%)
  matrix products  4.57 us (3%)
    all_gather x1, blocking collectives, shards(): combined_bias = lax.all_gather(partial_bias, 'axial', axis=1, tiled=True)  31 us
    all_gather x1, blocking collectives, shards(): lax.all_gather(factor_rows[:, :, factor_width:], 'axial', axis=1, tiled=T...  30.6 us
    reduce_scatter x1, waiting for transfers between devices, shards(): lax.psum_scatter(jnp.dot(arranged, outer_project_weight, preferred_elemen...  16.9 us
    all_to_all x1, starting transfers between devices, shards(): lax.all_to_all(lineup_embedding, 'axial', split_axis=0, concat_axis=1, ti...  7.4 us
    all_to_all x1, waiting for transfers between devices, shards(): lax.all_to_all(updated, 'axial', split_axis=1, concat_axis=0, tiled=True)  6.45 us
    all_to_all x1, starting transfers between devices, shards(): lax.all_to_all(updated, 'axial', split_axis=1, concat_axis=0, tiled=True)  5.44 us
    all_gather x1, blocking collectives, shards(): lax.all_gather(local_bias, ('branch', 'sub'), axis=2, tiled=True)  5.17 us
    unnamed x25, local copies, waits for them, and re-layouts  4.98 us
  transfers between devices with their start and end apart: 3, of which 2 were waited for; matrix products, arithmetic and copies ran while one was open for 3% of the time, Pallas kernels for 0%

commit v1 on v0

--- a/solution.py
+++ b/solution.py
@@ -1,6 +1,8 @@
 import jax
 import jax.numpy as jnp
 from jax import lax
+from jax.experimental import pallas as pl
+from jax.experimental.pallas import tpu as pltpu
 from jax.sharding import PartitionSpec as P
 
 HEAD_COUNT = 8
@@ -190,6 +192,314 @@
     return (back_rows, pair_delta_update)
 
 
+def iota(shape, dim):
+    return lax.broadcasted_iota(jnp.int32, shape, dim)
+
+
+def mm(a, b):
+    return jnp.dot(a, b, preferred_element_type=jnp.float32)
+
+
+def mm_t(a, b):
+    return lax.dot_general(a, b, (((1,), (1,)), ((), ())), preferred_element_type=jnp.float32)
+
+
+def one_hot(cond):
+    return jnp.where(cond, 1.0, 0.0).astype(jnp.bfloat16)
+
+
+def pick_lanes(cond, row):
+    return jnp.sum(jnp.where(cond, row, 0.0), axis=-1, keepdims=True)
+
+
+def fused_kernel(
+    own_ref,
+    pair_ref,
+    keep_ref,
+    mask_ref,
+    chain_ref,
+    intra_ref,
+    pbw_ref,
+    aw_hbm,
+    fw_hbm,
+    tw_hbm,
+    pw_hbm,
+    out_ref,
+    pair_out_ref,
+    msa,
+    bias_part,
+    bias_all,
+    aligned,
+    normed,
+    partial,
+    landed,
+    aw,
+    fw,
+    tw,
+    pw,
+    aw_t,
+    left_w,
+    right_w,
+    load_sem,
+    msa_send,
+    msa_recv,
+    part_send,
+    part_recv,
+    all_send,
+    all_recv,
+    sum_send,
+    sum_recv,
+):
+    f32, bf16 = jnp.float32, jnp.bfloat16
+    axial = lax.axis_index("axial")
+    n_axial = lax.axis_size("axial")
+    n_sub = lax.axis_size("sub")
+    group = lax.axis_index("branch") * n_sub + lax.axis_index("sub")
+    n_group = lax.axis_size("branch") * n_sub
+    axial_peers = [lax.rem(axial + d, n_axial) for d in range(n_axial)]
+    group_peers = [lax.rem(group + d, n_group) for d in range(n_group)]
+
+    def axial_id(d):
+        return {"axial": axial_peers[d]}
+
+    def group_id(d):
+        return {"branch": group_peers[d] // n_sub, "sub": group_peers[d] % n_sub}
+
+    barrier = pltpu.get_barrier_semaphore()
+    for d in range(1, n_axial):
+        pl.semaphore_signal(barrier, 1, device_id=axial_id(d), device_id_type=pl.DeviceIdType.MESH)
+    for d in range(1, n_group):
+        pl.semaphore_signal(barrier, 1, device_id=group_id(d), device_id_type=pl.DeviceIdType.MESH)
+    loads = [
+        pltpu.make_async_copy(src, dst, load_sem.at[n])
+        for n, (src, dst) in enumerate(((aw_hbm, aw), (fw_hbm, fw), (tw_hbm, tw), (pw_hbm, pw)))
+    ]
+    for load in loads:
+        load.start()
+
+    pair_rows = normalize_layer(pair_ref[...])
+    padded = jnp.concatenate([pair_rows] * 4, axis=0).astype(bf16)
+    local = mm(padded, pbw_ref[...]).T
+    lane = iota((32, 128), 1)
+    chain = jnp.broadcast_to(chain_ref[...].astype(f32), (8, 32)).astype(bf16)
+    chain_i = mm(chain, one_hot(iota((32, 128), 0) == axial * 4 + ((lane >> 3) & 3)))
+    chain_j = mm(chain, one_hot(iota((32, 128), 0) == group * 8 + (lane & 7)))
+    head_row = iota((8, 128), 0)
+    intra = jnp.zeros((8, 128), f32)
+    for h in range(HEAD_COUNT):
+        intra = jnp.where(head_row == h, intra_ref[h], intra)
+    local = local + jnp.where(chain_i == chain_j, intra, 0.0)
+    local = local.astype(bf16).astype(f32)
+    local = jnp.where((iota((8, 128), 1) >> 5) == group, local, 0.0)
+    bias_part[0] = local
+    msa[:, axial] = own_ref[...]
+
+    pl.semaphore_wait(barrier, n_axial + n_group - 2)
+    sends = []
+    for d in range(1, n_group):
+        copy = pltpu.make_async_remote_copy(
+            bias_part.at[0], bias_part.at[d], part_send.at[d], part_recv.at[d],
+            device_id=group_id(d), device_id_type=pl.DeviceIdType.MESH,
+        )
+        copy.start()
+        sends.append(copy)
+    part_copies = list(sends)
+    msa_copies = []
+    for d in range(1, n_axial):
+        copy = pltpu.make_async_remote_copy(
+            own_ref, msa.at[:, axial], msa_send.at[d], msa_recv.at[d],
+            device_id=axial_id(d), device_id_type=pl.DeviceIdType.MESH,
+        )
+        copy.start()
+        sends.append(copy)
+        msa_copies.append(copy)
+
+    keep = keep_ref[...].astype(f32)
+    mask = mask_ref[...].astype(f32)
+    row = iota((256, 32), 0)
+    lane32 = iota((256, 32), 1)
+    row_mask = pick_lanes(lane32 == ((row >> 4) & 7) * 4 + (row & 3), mask)
+    row_keep = pick_lanes(lane32 == group * 8 + (row >> 7) * 4 + ((row >> 2) & 3), keep)
+    row_weight = row_keep * row_mask
+    key_mask = (row_mask[:128] - 1.0) * 1000000000.0
+    seq_count = jnp.sum(keep)
+    for part in range(1, n_group):
+        part_copies[part - 1].wait_recv()
+    combined = bias_part[0]
+    for part in range(1, n_group):
+        combined = combined + bias_part[part]
+    bias_all[axial] = combined
+    all_copies = []
+    for d in range(1, n_axial):
+        copy = pltpu.make_async_remote_copy(
+            bias_all.at[axial], bias_all.at[axial], all_send.at[d], all_recv.at[d],
+            device_id=axial_id(d), device_id_type=pl.DeviceIdType.MESH,
+        )
+        copy.start()
+        sends.append(copy)
+        all_copies.append(copy)
+
+    for load in loads:
+        load.wait()
+    for n, at in enumerate((0, 2, 3)):
+        aw_t[n * 256 : (n + 1) * 256, :] = aw[:, at * 256 : (at + 1) * 256].T
+    side = tw[...]
+    lanes = iota((64, 1024), 1)
+    left_w[...] = mm(side, one_hot(iota((64, 1024), 0) == (lanes >> 5))).astype(bf16)
+    right_w[...] = mm(side, one_hot(iota((64, 1024), 0) == 32 + (lanes & 31))).astype(bf16)
+    k_at, c_at = iota((128, 128), 0), iota((128, 128), 1)
+    key_pick = one_hot((k_at >> 4) * 4 + (k_at & 3) == (c_at >> 5) * 8 + (c_at & 7))
+    query_pick = ((c_at >> 3) & 3) == (k_at & 3)
+    same_sequence = ((k_at >> 2) & 3) == ((c_at >> 2) & 3)
+
+    for copy in msa_copies:
+        copy.wait_recv()
+    rows = msa[...].reshape(256, 256)
+    rows_normed = normalize_layer(rows).astype(bf16)
+    keys = mm(rows_normed, aw[:, 256:512]).astype(bf16)
+    fronts = mm_t(aw_t[...], rows_normed).astype(bf16)
+    gate_t = jax.nn.sigmoid(fronts[512:].astype(f32))
+
+    for copy in all_copies:
+        copy.wait_recv()
+    scaling = 1.0 / HEAD_SPAN**0.5
+    attended = [[], []]
+    for h in range(HEAD_COUNT):
+        spread = jnp.concatenate(
+            [jnp.broadcast_to(bias_all[a, h : h + 1, :], (16, 128)) for a in range(8)], axis=0
+        )
+        spread = jnp.where(query_pick, spread, 0.0).astype(bf16)
+        bias = jnp.where(same_sequence, mm_t(key_pick, spread), -1e30)
+        lo, hi = h * HEAD_SPAN, (h + 1) * HEAD_SPAN
+        for half in range(2):
+            at = slice(half * 128, (half + 1) * 128)
+            pieces = [fronts[lo:hi, at]]
+            if lo:
+                pieces.insert(0, jnp.zeros((lo, 128), bf16))
+            if hi < 256:
+                pieces.append(jnp.zeros((256 - hi, 128), bf16))
+            scores = mm(keys[at], jnp.concatenate(pieces, axis=0)) * scaling + bias + key_mask
+            raised = jnp.exp(scores - jnp.max(scores, axis=0, keepdims=True))
+            weights = raised * (1.0 / jnp.sum(raised, axis=0, keepdims=True))
+            attended[half].append(mm(fronts[256 + lo : 256 + hi, at], weights.astype(bf16)))
+    attended_t = jnp.concatenate(
+        [jnp.concatenate(attended[half], axis=0) for half in range(2)], axis=1
+    )
+    gated = (attended_t * gate_t).T.astype(bf16)
+    updated = (rows.astype(f32) + mm(gated, fw[...])).astype(bf16)
+    aligned[...] = updated.reshape(2, 8, 16, 256)
+    out_ref[...] = aligned[:, axial]
+    side_in = (normalize_layer(updated) * row_weight).astype(bf16)
+    normed[...] = side_in.reshape(2, 8, 16, 256)
+
+    own_side = normed[:, axial].reshape(32, 256)
+    r_at = iota((128, 32), 0)
+    own_pick = one_hot(iota((128, 32), 1) == ((r_at >> 2) & 7) * 4 + (r_at >> 5))
+    own_spread = mm(own_pick, own_side).astype(bf16)
+    projected = jnp.zeros((256, 128), f32)
+    for chunk in range(4):
+        at = slice(chunk * 256, (chunk + 1) * 256)
+        right = mm(side_in, right_w[:, at]).astype(bf16).astype(f32).reshape(2, 8, 2, 8, 256)
+        left = mm(own_spread, left_w[:, at]).astype(bf16).astype(f32).reshape(4, 2, 2, 8, 256)
+        outer = []
+        for i in range(4):
+            total = right[0, :, 0] * left[i, 0, 0][None]
+            for half, two in ((0, 1), (1, 0), (1, 1)):
+                total = total + right[half, :, two] * left[i, half, two][None]
+            outer.append(total.reshape(64, 256))
+        projected = projected + mm(jnp.concatenate(outer, axis=0).astype(bf16), pw[at, :])
+    tiles = projected.reshape(4, 8, 8, 128)
+    upper = iota((8, 128), 0) < 4
+    for g in range(4):
+        for i in range(4):
+            one, two = tiles[i, 2 * g], tiles[i, 2 * g + 1]
+            one = one + pltpu.roll(one, 4, 0)
+            two = two + pltpu.roll(two, 4, 0)
+            partial[g, i] = jnp.where(upper, one, two)
+    sum_copies = []
+    for d in range(1, n_group):
+        copy = pltpu.make_async_remote_copy(
+            partial.at[group_peers[d]], landed.at[d], sum_send.at[d], sum_recv.at[d],
+            device_id=group_id(d), device_id_type=pl.DeviceIdType.MESH,
+        )
+        copy.start()
+        sends.append(copy)
+        sum_copies.append(copy)
+    small_lane = iota((8, 32), 1)
+    col_mask = pick_lanes(small_lane == group * 8 + iota((8, 32), 0), mask)
+    counts = [
+        jnp.maximum(seq_count * pick_lanes(small_lane == axial * 4 + i, mask) * col_mask, 1.0)
+        for i in range(4)
+    ]
+    for copy in sum_copies:
+        copy.wait_recv()
+    total = partial[group] + landed[1] + landed[2] + landed[3]
+    for i in range(4):
+        pair_out_ref[i] = (total[i] / counts[i]).astype(bf16)
+    for copy in sends:
+        copy.wait_send()
+
+
+def fused(lineup, pair, keep, mask, chain, intra, pbw, aw, fw, tw, pw):
+    f32, bf16 = jnp.float32, jnp.bfloat16
+    vmem = pl.BlockSpec(memory_space=pltpu.VMEM)
+    anywhere = pl.BlockSpec(memory_space=pl.ANY)
+    dma = pltpu.SemaphoreType.DMA
+    out, pair_out = pl.pallas_call(
+        fused_kernel,
+        out_shape=(
+            jax.ShapeDtypeStruct((2, 16, 256), bf16),
+            jax.ShapeDtypeStruct((4, 8, 128), bf16),
+        ),
+        in_specs=[vmem] * 5 + [pl.BlockSpec(memory_space=pltpu.SMEM), vmem] + [anywhere] * 4,
+        out_specs=(vmem, vmem),
+        scratch_shapes=[
+            pltpu.VMEM((2, 8, 16, 256), bf16),
+            pltpu.VMEM((4, 8, 128), f32),
+            pltpu.VMEM((8, 8, 128), f32),
+            pltpu.VMEM((2, 8, 16, 256), bf16),
+            pltpu.VMEM((2, 8, 16, 256), bf16),
+            pltpu.VMEM((4, 4, 8, 128), f32),
+            pltpu.VMEM((4, 4, 8, 128), f32),
+            pltpu.VMEM(aw.shape, bf16),
+            pltpu.VMEM(fw.shape, bf16),
+            pltpu.VMEM(tw.shape, bf16),
+            pltpu.VMEM(pw.shape, bf16),
+            pltpu.VMEM((768, 256), bf16),
+            pltpu.VMEM((256, 1024), bf16),
+            pltpu.VMEM((256, 1024), bf16),
+            dma((4,)),
+            dma((8,)), dma((8,)),
+            dma((4,)), dma((4,)),
+            dma((8,)), dma((8,)),
+            dma((4,)), dma((4,)),
+        ],
+        compiler_params=pltpu.CompilerParams(
+            collective_id=0, has_side_effects=True, vmem_limit_bytes=32 * 1024 * 1024
+        ),
+    )(
+        lineup.reshape(2, 16, 256),
+        pair.reshape(32, 128),
+        keep.reshape(1, 32),
+        mask.reshape(1, 32),
+        chain.reshape(1, 32),
+        intra,
+        pbw,
+        aw,
+        fw,
+        tw,
+        pw,
+    )
+    return out.reshape(lineup.shape), pair_out
+
+
+def per_device(lineup, pair, *rest):
+    axial, groups = lax.axis_size("axial"), lax.axis_size(("branch", "sub"))
+    small = lineup.shape == (8, 4, 256) and pair.shape == (4, 8, 128)
+    body = fused if small and axial == 8 and groups == 4 else shards
+    return body(lineup, pair, *rest)
+
+
 def solution(mesh):
     in_specs = (
         P(("branch", "sub"), "axial", None),
@@ -205,4 +515,6 @@
         P(),
     )
     out_specs = (P(("branch", "sub"), "axial", None), P("axial", ("branch", "sub"), None))
-    return jax.shard_map(shards, mesh=mesh, in_specs=in_specs, out_specs=out_specs, check_vma=False)
+    return jax.shard_map(
+        per_device, mesh=mesh, in_specs=in_specs, out_specs=out_specs, check_vma=False
+    )

time: 138 us -> 26.4 us (0.19)
  blocking collectives: 66.8 us -> 0 us
  waiting for transfers between devices: 23.4 us -> 0 us
  Pallas kernels: 0 us -> 19.7 us
  between operations: 14.3 us -> 0.74 us
  starting transfers between devices: 12.9 us -> 0 us
  other arithmetic: 5.54 us -> 0 us
  matrix products: 4.57 us -> 0 us
  local copies, waits for them, and re-layouts: 9.87 us -> 5.69 us
    all_gather x3 -> x0, blocking collectives: 66.8 us -> none  [the longest x1 31 us: shards(): combined_bias = lax.all_gather(partial_bias, 'axial', axis=1, tiled=True)]
    pallas_call x0 -> x1, Pallas kernels: none -> 19.7 us  [fused(): pl.pallas_call(fused_kernel, out_shape=(jax.ShapeDtypeStruct((2, 16, 256)...]
    reduce_scatter x1 -> x0, waiting for transfers between devices: 16.9 us -> none  [shards(): lax.psum_scatter(jnp.dot(arranged, outer_project_weight, preferred_elemen...]
    all_to_all x2 -> x0, starting transfers between devices: 12.8 us -> none  [the longest x1 7.4 us: shards(): lax.all_to_all(lineup_embedding, 'axial', split_axis=0, concat_axis=1, ti...]
    all_to_all x2 -> x0, waiting for transfers between devices: 6.45 us -> none  [the longest x1 6.45 us: shards(): lax.all_to_all(updated, 'axial', split_axis=1, concat_axis=0, tiled=True)]
    dot_general x23 -> x0, matrix products: 4.57 us -> none  [the longest x8 1.49 us: one_head(): jnp.einsum('sqk,skd->sqd', weights, val_side, preferred_element_type=jnp....]
    reduce_sum x15 -> x0, other arithmetic: 2.15 us -> none  [the longest x3 0.83 us: normalize_layer(): variance = jnp.mean(centered * centered, axis=-1, keepdims=True)]
    convert_element_type x6 -> x0, other arithmetic: 1.75 us -> none  [the longest x1 1.39 us: shards(): (pair_sums / jnp.maximum(counted, 1.0)[:, :, None]).astype(jnp.bfloat16)]
  transfers between devices with their start and end apart: 3 -> 0, of which waited for: 2 -> 0; matrix products, arithmetic and copies ran while one was open for 3% -> 0% of each run, Pallas kernels for 0% -> 0%
where the time goes in v1:
time: 26.4 us; the launch traced here: 26.1 us
  Pallas kernels  19.7 us (75%)
  local copies, waits for them, and re-layouts  5.69 us (22%)
  between operations  0.74 us (3%)
    pallas_call x1, Pallas kernels, fused(): pl.pallas_call(fused_kernel, out_shape=(jax.ShapeDtypeStruct((2, 16, 256)...  19.7 us
    unnamed x19, local copies, waits for them, and re-layouts  4.31 us
    reshape x1, local copies, waits for them, and re-layouts, fused(): lineup.reshape(2, 16, 256)  0.76 us
    reshape x1, local copies, waits for them, and re-layouts, fused(): return (out.reshape(lineup.shape), pair_out)  0.62 us

profile of v1, /device:TPU:0, one launch (start us, length us, event | category | flops | bytes accessed | tf_op | source)
XLA Modules:
  0.0 26.1 jit_solution(1013648733910324766)
XLA Ops:
  0.6 0.0 copy-start.2
  0.6 0.8 %reshape.22.own_ref = bf16[2,16,256]{2,1,0:T(8,128)(2,1)S(1)} reshape(bf16[8,4,256]{2,1,0:T(4,128)(2,1)} %param.11) | data formatting | bytes 32768 | tf_op jit(solution)/shard_map/reshape | solution.py:481
  1.4 0.8 %copy.13.pbw_ref = bf16[128,8]{1,0:T(8,128)(2,1)S(1)} copy(bf16[128,8]{0,1:T(8,128)(2,1)} %param.17) | data formatting | bytes 4096 | tf_op args[6]
  2.2 0.0 copy-start.3
  2.2 0.0 copy-start.4
  2.2 0.0 copy-start.5
  2.2 0.0 copy-start.6
  2.2 0.0 copy-start.7
  2.3 0.9 %copy.14.tw_hbm = bf16[256,64]{1,0:T(8,128)(2,1)S(1)} copy(bf16[256,64]{0,1:T(8,128)(2,1)} %param.20) | data formatting | bytes 65536 | tf_op args[9]
  3.2 0.0 copy-done.2
  3.2 0.0 copy-done.3
  3.2 0.0 copy-done.4
  3.2 0.0 copy-done.5
  3.2 0.0 copy-done.6
  3.2 0.0 copy-done.7
  3.2 0.0 copy-start
  3.2 1.0 %copy-done = bf16[256,1024]{1,0:T(8,128)(2,1)S(1)} copy-done((bf16[256,1024]{1,0:T(8,128)(2,1)S(1)}, bf16[256,1024]{1,0:T(8,128)(2,1)}, u32[]{:S(2)}) %copy-start) | copy-done | bytes 524312
  4.3 0.0 copy-start.1
  4.3 0.9 %copy-done.1 = bf16[1024,128]{1,0:T(8,128)(2,1)S(1)} copy-done((bf16[1024,128]{1,0:T(8,128)(2,1)S(1)}, bf16[1024,128]{1,0:T(8,128)(2,1)}, u32[]{:S(2)}) %copy-start.1) | copy-done | bytes 262168
  5.2 19.7 %shard_map.122 = (bf16[2,16,256]{2,1,0:T(8,128)(2,1)S(1)}, bf16[4,8,128]{2,1,0:T(8,128)(2,1)S(1)}) custom-call(bf16[2,16,256]{2,1,0:T(8,128)(2,1)S(1)} %reshape.22.own_ref, bf16[32,128]{1,0:T(8,128)(2,1)S(1)} %bitcast.4, s32[1,32]{1,0:T(1,128)S(1)} %bitcast.5, s32[1,32]{1,0:T(1,128)S(1)} %bitcast.6, s32[1,32]{1,0:T(1,128)S(1)} %bitcast.7, f32[8]{0:T(128)S(1)} %copy-done.7, ...), custom_call_target="tpu_custom_call" | custom-call | tf_op jit(solution)/shard_map/pallas_call | solution.py:448
  24.9 0.6 %reshape.27 = bf16[8,4,256]{2,1,0:T(4,128)(2,1)} reshape(bf16[2,16,256]{2,1,0:T(8,128)(2,1)S(1)} %get-tuple-element.4) | data formatting | bytes 32768 | tf_op jit(solution)/shard_map/reshape | solution.py:493
  25.5 0.6 %copy.16 = bf16[4,8,128]{2,1,0:T(8,128)(2,1)} copy(bf16[4,8,128]{2,1,0:T(8,128)(2,1)S(1)} %get-tuple-element.9) | data formatting | bytes 16384
Async XLA Ops:
  0.6 2.5 %copy-start.2 = (bf16[256,256]{1,0:T(8,128)(2,1)S(1)}, bf16[256,256]{1,0:T(8,128)(2,1)}, u32[]{:S(2)}) copy-start(bf16[256,256]{1,0:T(8,128)(2,1)} %fw_hbm.1) | copy-start | bytes 393220
  2.2 1.0 %copy-start.3 = (bf16[4,8,128]{2,1,0:T(8,128)(2,1)S(1)}, bf16[4,8,128]{2,1,0:T(8,128)(2,1)}, u32[]{:S(2)}) copy-start(bf16[4,8,128]{2,1,0:T(8,128)(2,1)} %param.12) | copy-start | bytes 24580
  2.2 1.0 %copy-start.4 = (s32[32]{0:T(128)S(1)}, s32[32]{0:T(128)}, u32[]{:S(2)}) copy-start(s32[32]{0:T(128)} %param.13) | copy-start | bytes 388
  2.2 1.0 %copy-start.5 = (s32[32]{0:T(128)S(1)}, s32[32]{0:T(128)}, u32[]{:S(2)}) copy-start(s32[32]{0:T(128)} %param.14) | copy-start | bytes 388
  2.2 1.0 %copy-start.6 = (s32[32]{0:T(128)S(1)}, s32[32]{0:T(128)}, u32[]{:S(2)}) copy-start(s32[32]{0:T(128)} %param.15) | copy-start | bytes 388
  2.2 1.0 %copy-start.7 = (f32[8]{0:T(128)S(1)}, f32[8]{0:T(128)}, u32[]{:S(2)}) copy-start(f32[8]{0:T(128)} %intra_ref.1) | copy-start | bytes 100
  3.2 1.0 %copy-start = (bf16[256,1024]{1,0:T(8,128)(2,1)S(1)}, bf16[256,1024]{1,0:T(8,128)(2,1)}, u32[]{:S(2)}) copy-start(bf16[256,1024]{1,0:T(8,128)(2,1)} %aw_hbm.1) | copy-start | bytes 1572868
  4.3 0.9 %copy-start.1 = (bf16[1024,128]{1,0:T(8,128)(2,1)S(1)}, bf16[1024,128]{1,0:T(8,128)(2,1)}, u32[]{:S(2)}) copy-start(bf16[1024,128]{1,0:T(8,128)(2,1)} %pw_hbm.1) | copy-start | bytes 786436

commit v2 on v1

--- a/solution.py
+++ b/solution.py
@@ -213,6 +213,19 @@
 
 
 def fused_kernel(
+    own_hbm,
+    pair_hbm,
+    keep_hbm,
+    mask_hbm,
+    chain_hbm,
+    intra_hbm,
+    pbw_hbm,
+    aw_hbm,
+    fw_hbm,
+    tw_hbm,
+    pw_hbm,
+    out_ref,
+    pair_out_ref,
     own_ref,
     pair_ref,
     keep_ref,
@@ -220,12 +233,6 @@
     chain_ref,
     intra_ref,
     pbw_ref,
-    aw_hbm,
-    fw_hbm,
-    tw_hbm,
-    pw_hbm,
-    out_ref,
-    pair_out_ref,
     msa,
     bias_part,
     bias_all,
@@ -265,21 +272,39 @@
     def group_id(d):
         return {"branch": group_peers[d] // n_sub, "sub": group_peers[d] % n_sub}
 
+    loads = [
+        pltpu.make_async_copy(src, dst, load_sem.at[n])
+        for n, (src, dst) in enumerate(
+            (
+                (pair_hbm, pair_ref),
+                (pbw_hbm, pbw_ref),
+                (chain_hbm, chain_ref),
+                (intra_hbm, intra_ref),
+                (own_hbm, own_ref),
+                (keep_hbm, keep_ref),
+                (mask_hbm, mask_ref),
+                (aw_hbm, aw),
+                (tw_hbm, tw),
+                (fw_hbm, fw),
+                (pw_hbm, pw),
+            )
+        )
+    ]
+    for load in loads[:5]:
+        load.start()
     barrier = pltpu.get_barrier_semaphore()
     for d in range(1, n_axial):
         pl.semaphore_signal(barrier, 1, device_id=axial_id(d), device_id_type=pl.DeviceIdType.MESH)
     for d in range(1, n_group):
         pl.semaphore_signal(barrier, 1, device_id=group_id(d), device_id_type=pl.DeviceIdType.MESH)
-    loads = [
-        pltpu.make_async_copy(src, dst, load_sem.at[n])
-        for n, (src, dst) in enumerate(((aw_hbm, aw), (fw_hbm, fw), (tw_hbm, tw), (pw_hbm, pw)))
-    ]
-    for load in loads:
+    for load in loads[5:]:
         load.start()
+    for load in loads[:5]:
+        load.wait()
 
     pair_rows = normalize_layer(pair_ref[...])
     padded = jnp.concatenate([pair_rows] * 4, axis=0).astype(bf16)
-    local = mm(padded, pbw_ref[...]).T
+    local = mm_t(pbw_ref[...], padded)
     lane = iota((32, 128), 1)
     chain = jnp.broadcast_to(chain_ref[...].astype(f32), (8, 32)).astype(bf16)
     chain_i = mm(chain, one_hot(iota((32, 128), 0) == axial * 4 + ((lane >> 3) & 3)))
@@ -292,7 +317,7 @@
     local = local.astype(bf16).astype(f32)
     local = jnp.where((iota((8, 128), 1) >> 5) == group, local, 0.0)
     bias_part[0] = local
-    msa[:, axial] = own_ref[...]
+    msa[:, axial] = own_ref[...].astype(f32).reshape(2, 16, 256).astype(bf16)
 
     pl.semaphore_wait(barrier, n_axial + n_group - 2)
     sends = []
@@ -307,13 +332,15 @@
     msa_copies = []
     for d in range(1, n_axial):
         copy = pltpu.make_async_remote_copy(
-            own_ref, msa.at[:, axial], msa_send.at[d], msa_recv.at[d],
+            msa.at[:, axial], msa.at[:, axial], msa_send.at[d], msa_recv.at[d],
             device_id=axial_id(d), device_id_type=pl.DeviceIdType.MESH,
         )
         copy.start()
         sends.append(copy)
         msa_copies.append(copy)
 
+    for load in loads[5:7]:
+        load.wait()
     keep = keep_ref[...].astype(f32)
     mask = mask_ref[...].astype(f32)
     row = iota((256, 32), 0)
@@ -339,14 +366,14 @@
         sends.append(copy)
         all_copies.append(copy)
 
-    for load in loads:
+    for load in loads[7:]:
         load.wait()
     for n, at in enumerate((0, 2, 3)):
         aw_t[n * 256 : (n + 1) * 256, :] = aw[:, at * 256 : (at + 1) * 256].T
     side = tw[...]
-    lanes = iota((64, 1024), 1)
-    left_w[...] = mm(side, one_hot(iota((64, 1024), 0) == (lanes >> 5))).astype(bf16)
-    right_w[...] = mm(side, one_hot(iota((64, 1024), 0) == 32 + (lanes & 31))).astype(bf16)
+    rank, channel = iota((1024, 64), 0), iota((1024, 64), 1)
+    left_w[...] = mm(one_hot(channel == (rank >> 5)), side).astype(bf16)
+    right_w[...] = mm(one_hot(channel == 32 + (rank & 31)), side).astype(bf16)
     k_at, c_at = iota((128, 128), 0), iota((128, 128), 1)
     key_pick = one_hot((k_at >> 4) * 4 + (k_at & 3) == (c_at >> 5) * 8 + (c_at & 7))
     query_pick = ((c_at >> 3) & 3) == (k_at & 3)
@@ -388,7 +415,7 @@
     gated = (attended_t * gate_t).T.astype(bf16)
     updated = (rows.astype(f32) + mm(gated, fw[...])).astype(bf16)
     aligned[...] = updated.reshape(2, 8, 16, 256)
-    out_ref[...] = aligned[:, axial]
+    out_ref[...] = aligned[:, axial].astype(f32).reshape(8, 4, 256).astype(bf16)
     side_in = (normalize_layer(updated) * row_weight).astype(bf16)
     normed[...] = side_in.reshape(2, 8, 16, 256)
 
@@ -399,8 +426,8 @@
     projected = jnp.zeros((256, 128), f32)
     for chunk in range(4):
         at = slice(chunk * 256, (chunk + 1) * 256)
-        right = mm(side_in, right_w[:, at]).astype(bf16).astype(f32).reshape(2, 8, 2, 8, 256)
-        left = mm(own_spread, left_w[:, at]).astype(bf16).astype(f32).reshape(4, 2, 2, 8, 256)
+        right = mm_t(side_in, right_w[at]).astype(bf16).astype(f32).reshape(2, 8, 2, 8, 256)
+        left = mm_t(own_spread, left_w[at]).astype(bf16).astype(f32).reshape(4, 2, 2, 8, 256)
         outer = []
         for i in range(4):
             total = right[0, :, 0] * left[i, 0, 0][None]
@@ -443,17 +470,24 @@
 def fused(lineup, pair, keep, mask, chain, intra, pbw, aw, fw, tw, pw):
     f32, bf16 = jnp.float32, jnp.bfloat16
     vmem = pl.BlockSpec(memory_space=pltpu.VMEM)
-    anywhere = pl.BlockSpec(memory_space=pl.ANY)
+    hbm = pl.BlockSpec(memory_space=pltpu.HBM)
     dma = pltpu.SemaphoreType.DMA
     out, pair_out = pl.pallas_call(
         fused_kernel,
         out_shape=(
-            jax.ShapeDtypeStruct((2, 16, 256), bf16),
+            jax.ShapeDtypeStruct(lineup.shape, bf16),
             jax.ShapeDtypeStruct((4, 8, 128), bf16),
         ),
-        in_specs=[vmem] * 5 + [pl.BlockSpec(memory_space=pltpu.SMEM), vmem] + [anywhere] * 4,
+        in_specs=[hbm] * 11,
         out_specs=(vmem, vmem),
         scratch_shapes=[
+            pltpu.VMEM(lineup.shape, bf16),
+            pltpu.VMEM((32, 128), bf16),
+            pltpu.VMEM((1, 32), jnp.int32),
+            pltpu.VMEM((1, 32), jnp.int32),
+            pltpu.VMEM((1, 32), jnp.int32),
+            pltpu.SMEM((HEAD_COUNT,), f32),
+            pltpu.VMEM((HEAD_COUNT, 128), bf16),
             pltpu.VMEM((2, 8, 16, 256), bf16),
             pltpu.VMEM((4, 8, 128), f32),
             pltpu.VMEM((8, 8, 128), f32),
@@ -463,34 +497,34 @@
             pltpu.VMEM((4, 4, 8, 128), f32),
             pltpu.VMEM(aw.shape, bf16),
             pltpu.VMEM(fw.shape, bf16),
-            pltpu.VMEM(tw.shape, bf16),
+            pltpu.VMEM((64, 256), bf16),
             pltpu.VMEM(pw.shape, bf16),
             pltpu.VMEM((768, 256), bf16),
-            pltpu.VMEM((256, 1024), bf16),
-            pltpu.VMEM((256, 1024), bf16),
-            dma((4,)),
+            pltpu.VMEM((1024, 256), bf16),
+            pltpu.VMEM((1024, 256), bf16),
+            dma((11,)),
             dma((8,)), dma((8,)),
             dma((4,)), dma((4,)),
             dma((8,)), dma((8,)),
             dma((4,)), dma((4,)),
         ],
         compiler_params=pltpu.CompilerParams(
-            collective_id=0, has_side_effects=True, vmem_limit_bytes=32 * 1024 * 1024
+            collective_id=0, has_side_effects=True, vmem_limit_bytes=56 * 1024 * 1024
         ),
     )(
-        lineup.reshape(2, 16, 256),
+        lineup,
         pair.reshape(32, 128),
         keep.reshape(1, 32),
         mask.reshape(1, 32),
         chain.reshape(1, 32),
         intra,
-        pbw,
+        pbw.T,
         aw,
         fw,
-        tw,
+        tw.T,
         pw,
     )
-    return out.reshape(lineup.shape), pair_out
+    return out, pair_out
 
 
 def per_device(lineup, pair, *rest):

time: 26.4 us -> 22.2 us (0.84)
  local copies, waits for them, and re-layouts: 5.69 us -> 1.94 us
  Pallas kernels: 19.7 us -> 19.4 us
    unnamed x19 -> x4, local copies, waits for them, and re-layouts: 4.31 us -> 1.94 us
    reshape x2 -> x0, local copies, waits for them, and re-layouts: 1.38 us -> none  [the longest x1 0.76 us: fused(): lineup.reshape(2, 16, 256)]
where the time goes in v2:
time: 22.2 us; the launch traced here: 22 us
  Pallas kernels  19.4 us (87%)
  local copies, waits for them, and re-layouts  1.94 us (9%)
  between operations  0.65 us (3%)
    pallas_call x1, Pallas kernels, fused(): pl.pallas_call(fused_kernel, out_shape=(jax.ShapeDtypeStruct(lineup.shape...  19.4 us
    unnamed x4, local copies, waits for them, and re-layouts  1.94 us

profile of v2, /device:TPU:0, one launch (start us, length us, event | category | flops | bytes accessed | tf_op | source)
XLA Modules:
  0.0 22.0 jit_solution(6294547737458894654)
XLA Ops:
  0.6 19.4 %shard_map.122 = (bf16[8,4,256]{2,1,0:T(4,128)(2,1)}, bf16[4,8,128]{2,1,0:T(8,128)(2,1)}) custom-call(bf16[8,4,256]{2,1,0:T(4,128)(2,1)} %own_hbm.1, bf16[32,128]{1,0:T(8,128)(2,1)} %bitcast.7, s32[1,32]{1,0:T(1,128)} %bitcast.9, s32[1,32]{1,0:T(1,128)} %bitcast.10, s32[1,32]{1,0:T(1,128)} %bitcast.11, f32[8]{0:T(128)} %intra_hbm.1, bf16[8,128]{1,0:T(8,128)(2,1)} %bitcast.8, ...), custom_call_target="tpu_custom_call" | custom-call | tf_op jit(solution)/shard_map/pallas_call | solution.py:475
  20.1 0.0 copy-start
  20.1 1.3 %copy.15 = bf16[8,4,256]{2,1,0:T(4,128)(2,1)} copy(bf16[8,4,256]{2,1,0:T(4,128)(2,1)} %get-tuple-element.4) | data formatting | bytes 32768
  21.4 0.0 copy-done
  21.4 0.6 %copy.16 = bf16[4,8,128]{2,1,0:T(8,128)(2,1)} copy(bf16[4,8,128]{2,1,0:T(8,128)(2,1)S(1)} %copy-done) | data formatting | bytes 16384
Async XLA Ops:
  20.1 1.3 %copy-start = (bf16[4,8,128]{2,1,0:T(8,128)(2,1)S(1)}, bf16[4,8,128]{2,1,0:T(8,128)(2,1)}, u32[]{:S(2)}) copy-start(bf16[4,8,128]{2,1,0:T(8,128)(2,1)} %get-tuple-element.5) | copy-start | bytes 24580

commit v3 on v2

--- a/solution.py
+++ b/solution.py
@@ -290,14 +290,12 @@
             )
         )
     ]
-    for load in loads[:5]:
-        load.start()
     barrier = pltpu.get_barrier_semaphore()
     for d in range(1, n_axial):
         pl.semaphore_signal(barrier, 1, device_id=axial_id(d), device_id_type=pl.DeviceIdType.MESH)
     for d in range(1, n_group):
         pl.semaphore_signal(barrier, 1, device_id=group_id(d), device_id_type=pl.DeviceIdType.MESH)
-    for load in loads[5:]:
+    for load in loads:
         load.start()
     for load in loads[:5]:
         load.wait()

time: 22.2 us -> 22.2 us (level)
  no operation moved by 1% of the time
where the time goes in v3:
time: 22.2 us; the launch traced here: 22 us
  Pallas kernels  19.4 us (87%)
  local copies, waits for them, and re-layouts  1.94 us (9%)
  between operations  0.65 us (3%)
    pallas_call x1, Pallas kernels, fused(): pl.pallas_call(fused_kernel, out_shape=(jax.ShapeDtypeStruct(lineup.shape...  19.4 us
    unnamed x4, local copies, waits for them, and re-layouts  1.94 us

profile of v3, /device:TPU:0, one launch (start us, length us, event | category | flops | bytes accessed | tf_op | source)
XLA Modules:
  0.0 22.0 jit_solution(736477736498389739)
XLA Ops:
  0.6 19.4 %shard_map.122 = (bf16[8,4,256]{2,1,0:T(4,128)(2,1)}, bf16[4,8,128]{2,1,0:T(8,128)(2,1)}) custom-call(bf16[8,4,256]{2,1,0:T(4,128)(2,1)} %own_hbm.1, bf16[32,128]{1,0:T(8,128)(2,1)} %bitcast.7, s32[1,32]{1,0:T(1,128)} %bitcast.9, s32[1,32]{1,0:T(1,128)} %bitcast.10, s32[1,32]{1,0:T(1,128)} %bitcast.11, f32[8]{0:T(128)} %intra_hbm.1, bf16[8,128]{1,0:T(8,128)(2,1)} %bitcast.8, ...), custom_call_target="tpu_custom_call" | custom-call | tf_op jit(solution)/shard_map/pallas_call | solution.py:473
  20.1 0.0 copy-start
  20.1 1.3 %copy.15 = bf16[8,4,256]{2,1,0:T(4,128)(2,1)} copy(bf16[8,4,256]{2,1,0:T(4,128)(2,1)} %get-tuple-element.4) | data formatting | bytes 32768
  21.4 0.0 copy-done
  21.4 0.6 %copy.16 = bf16[4,8,128]{2,1,0:T(8,128)(2,1)} copy(bf16[4,8,128]{2,1,0:T(8,128)(2,1)S(1)} %copy-done) | data formatting | bytes 16384
Async XLA Ops:
  20.1 1.3 %copy-start = (bf16[4,8,128]{2,1,0:T(8,128)(2,1)S(1)}, bf16[4,8,128]{2,1,0:T(8,128)(2,1)}, u32[]{:S(2)}) copy-start(bf16[4,8,128]{2,1,0:T(8,128)(2,1)} %get-tuple-element.5) | copy-start | bytes 24580
